TPU v7x, 32 devices: a whole 2x2x4 slice. The times are simulated.
32 devices in a mesh: prod: 8 (over y, x, core), pre: 4 (over z).
Axes of the slice: x: 2, y: 2, z: 4, core: 2. Of those that a mesh axis runs over, the one named last changes fastest.
Arguments:
- potentials: bfloat16 [128, 16, 512], P(('prod', 'pre')), may hold values from -6 to 6
- injected: float32 [128, 16, 512], P(('prod', 'pre')), may hold values from -6 to 6
- near_blocks: bfloat16 [128, 4, 512, 512], P('prod', 'pre'), may hold values from -0.125 to 0.125
- near_cols: int32 [128, 4], P('prod', 'pre'), may hold values from 0 to 127, as said below
- row_basis: bfloat16 [128, 16, 512], P('prod'), may hold values from -1.5 to 1.5
- col_basis: bfloat16 [128, 16, 512], P(('prod', 'pre')), may hold values from -0.25 to 0.25
- basis_ranks: int32 [128], P(('prod', 'pre')), may hold values from 1 to 16
- couplings: bfloat16 [128, 16, 2048], P('prod', None, 'pre'), may hold values from -0.125 to 0.125
- inverses: bfloat16 [128, 512, 512], P(('prod', 'pre')), may hold values from -0.25 to 0.25
Outputs:
- residual: float32 [128, 16, 512], P(('prod', 'pre'))
- corrected: float32 [128, 16, 512], P(('prod', 'pre'))
Inputs may be any that keep to these rules, and one draw needn't show every extreme that they name: near_cols[i, 0] = i; near_cols[i, 1] is i + 8 or i - 8; every other entry differs from i by 1 to 7.
All inputs are finite; a program needn't handle non-finite values.
Results may differ from a plain program's by a relative error of at most 0.012.
Values may be sent and summed in bfloat16 or wider, within the bound.
A program may use at most 64 MiB of HBM per device.

v0:
```python
import functools

import jax
import jax.numpy as jnp
from jax import lax
from jax.experimental import pallas as pl
from jax.experimental.pallas import tpu as pltpu
from jax.sharding import PartitionSpec as P

MESH = pl.DeviceIdType.MESH
NT = (((1,), (1,)), ((), ()))


def kernel(
    n_prod,
    n_pre,
    pot_hbm,
    inj_hbm,
    near_hbm,
    cols_ref,
    rowb_hbm,
    colb_hbm,
    ranks_ref,
    coup_hbm,
    inv_hbm,
    res_ref,
    cor_ref,
    group,
    soon,
    late,
    inj,
    near,
    rowb,
    colb,
    coup,
    inv,
    coef,
    far,
    mine,
    res,
    cor,
    sending,
    arriving,
    load_sem,
    near_sem,
    gather_send,
    gather_recv,
    halo_send,
    halo_recv,
    coef_send,
    coef_recv,
    part_send,
    part_recv,
    out_sem,
):
    owned, scen, panels = pot_hbm.shape
    rows = near_hbm.shape[0]
    rank_cap = colb_hbm.shape[1]
    half_rows = rows // 2
    half = n_pre // 2
    width = owned * rank_cap
    p = lax.axis_index("prod")
    z = lax.axis_index("pre")
    high, low = z // half, z % half
    others = [(1 - high) * half + (low + e) % half for e in range(half)]
    others += [high * half + (low + e) % half for e in range(1, half)]
    nearest = others[half:] + others[:half]

    def slot(first):
        return group.at[pl.ds(first * owned, owned)]

    load_pot = pltpu.make_async_copy(pot_hbm, slot(z), load_sem.at[0])
    load_colb = pltpu.make_async_copy(colb_hbm, colb, load_sem.at[1])
    load_coup = pltpu.make_async_copy(coup_hbm, coup, load_sem.at[2])
    load_rowb = pltpu.make_async_copy(rowb_hbm, rowb, load_sem.at[3])
    load_inj = pltpu.make_async_copy(inj_hbm, inj, load_sem.at[4])
    load_inv = pltpu.make_async_copy(inv_hbm, inv, load_sem.at[5])
    load_pot.start()
    load_colb.start()

    barrier = pltpu.get_barrier_semaphore()
    for target in others:
        pl.semaphore_signal(barrier, inc=1, device_id=(p, target), device_id_type=MESH)
    for e in range(1, n_prod):
        pl.semaphore_signal(
            barrier, inc=1, device_id=((p + e) % n_prod, z), device_id_type=MESH
        )
    pl.semaphore_wait(barrier, n_pre - 1 + n_prod - 1)

    gathers = []
    for e, target in enumerate(others):
        gathers.append(
            pltpu.make_async_remote_copy(
                src_ref=pot_hbm,
                dst_ref=slot(z),
                send_sem=gather_send.at[e],
                recv_sem=gather_recv.at[z],
                device_id=(p, target),
                device_id_type=MESH,
            )
        )
        gathers[-1].start()

    halos = []
    odd = p % 2
    mate, side = p + 1 - 2 * odd, 1 - odd

    def halo_copy(buffer, zs, send, source, to):
        return pltpu.make_async_remote_copy(
            src_ref=source,
            dst_ref=buffer.at[pl.ds(zs % half * owned, owned)],
            send_sem=halo_send.at[send],
            recv_sem=halo_recv.at[zs],
            device_id=(to, z),
            device_id_type=MESH,
        )

    def forward(zs, index, source=None):
        source = slot(zs) if source is None else source
        to = jnp.where(zs < half, p - 1, p + 1)
        near_by = (z >= 1) & (to == mate)
        far_off = (z >= 1) & (to != mate) & (to >= 0) & (to < n_prod)
        for ok, buffer in ((near_by, soon), (far_off, late)):
            copy = halo_copy(buffer, zs, index, source, to)

            @pl.when(ok)
            def _():
                copy.start()

            halos.append((ok, copy))

    def await_halo(buffer, upper, from_device):
        @pl.when((z >= 1) & (from_device >= 0) & (from_device < n_prod))
        def _():
            for e in range(half):
                zs = (1 - upper) * half + e
                halo_copy(buffer, zs, 0, slot(zs), from_device).wait_recv()

    forward(z, 0, pot_hbm)
    load_coup.start()
    load_rowb.start()
    same = (side == high) & (z >= 1)
    cross, beside = others[:half], others[half:]
    orders = (cross + beside + [z], beside + cross + [z])

    def near_load(row):
        return pltpu.make_async_copy(near_hbm.at[row, 0], near.at[row], near_sem.at[row])

    for first, second in zip(*orders):
        for j in range(owned):
            near_load(jnp.where(same, second, first) * owned + j).start()
    load_inj.start()
    load_inv.start()
    load_pot.wait()
    load_colb.wait()

    pot = group[pl.ds(z * owned, owned)].reshape(owned * scen, panels)
    basis = colb[...].reshape(width, panels)
    products = lax.dot_general(
        pot,
        jnp.concatenate([basis] * (128 // width), axis=0),
        NT,
        preferred_element_type=jnp.float32,
    )
    lane = lax.broadcasted_iota(jnp.int32, (scen, 128), 1)
    inner = lane % width
    here = (lane // width) == p % (128 // width)
    mine_coef = jnp.zeros((scen, 128), jnp.float32)
    for j in range(owned):
        keep = here & (inner // rank_cap == j) & (inner % rank_cap < ranks_ref[j])
        mine_coef = jnp.where(keep, products[j * scen : (j + 1) * scen], mine_coef)
    coef[p] = mine_coef.astype(jnp.bfloat16)
    coef_copies = []
    for e in range(1, n_prod):
        coef_copies.append(
            pltpu.make_async_remote_copy(
                src_ref=coef.at[p],
                dst_ref=coef.at[p],
                send_sem=coef_send.at[e],
                recv_sem=coef_recv.at[p],
                device_id=((p + e) % n_prod, z),
                device_id_type=MESH,
            )
        )
        coef_copies[-1].start()

    def collect(index):
        zs = nearest[index]
        pltpu.make_async_remote_copy(
            src_ref=slot(zs),
            dst_ref=slot(zs),
            send_sem=gather_send.at[0],
            recv_sem=gather_recv.at[zs],
            device_id=(p, zs),
            device_id_type=MESH,
        ).wait_recv()
        forward(zs, index + 1)

    for index in range(n_pre - 1):
        collect(index)

    for e in range(1, n_prod):
        b = (p + e) % n_prod
        pltpu.make_async_remote_copy(
            src_ref=coef.at[b],
            dst_ref=coef.at[b],
            send_sem=coef_send.at[0],
            recv_sem=coef_recv.at[b],
            device_id=(b, z),
            device_id_type=MESH,
        ).wait_recv()
    load_coup.wait()
    load_rowb.wait()
    share = 128 // width
    blocks = []
    for m in range(n_prod // share):
        block = coef[m * share]
        for e in range(1, share):
            block = block + coef[m * share + e]
        blocks.append(block)
    columns = jnp.concatenate(blocks, axis=1)
    weights = lax.dot_general(
        columns,
        coup[...].reshape(rows * rank_cap, n_prod * width),
        NT,
        preferred_element_type=jnp.float32,
    )
    weights = jnp.concatenate([weights] * rows, axis=0)
    shape = (rows * scen, rows * rank_cap)
    row_of = lax.broadcasted_iota(jnp.int32, shape, 0) // scen
    col_of = lax.broadcasted_iota(jnp.int32, shape, 1) // rank_cap
    weights = jnp.where(row_of == col_of, weights, 0.0).astype(jnp.bfloat16)
    far[...] = jnp.dot(
        weights,
        rowb[...].reshape(rows * rank_cap, panels),
        preferred_element_type=jnp.float32,
    ).reshape(rows, scen, panels)

    offset = p * rows

    def partial_row(row, buffer, upper):
        index = cols_ref[row] - offset
        beyond = jnp.where(upper == 1, index - rows, index + half_rows)
        outside = (index < 0) | (index >= rows)
        picked = jnp.where(
            outside,
            buffer[jnp.clip(beyond, 0, half_rows - 1)],
            group[jnp.clip(index, 0, rows - 1)],
        )
        value = lax.dot_general(picked, near[row], NT, preferred_element_type=jnp.float32)
        return value + far[row]

    def part_copy(target):
        return pltpu.make_async_remote_copy(
            src_ref=sending.at[target],
            dst_ref=arriving.at[z],
            send_sem=part_send.at[target],
            recv_sem=part_recv.at[z],
            device_id=(p, target),
            device_id_type=MESH,
        )

    def rows_of(target, buffer, upper):
        return [partial_row(target * owned + j, buffer, upper) for j in range(owned)]

    def send_rows(targets, buffer, upper):
        for target in targets:
            for j, value in enumerate(rows_of(target, buffer, upper)):
                sending[target, j] = value.astype(jnp.bfloat16)
            part_copy(target).start()

    def keep_rows(buffer, upper):
        for j, value in enumerate(rows_of(z, buffer, upper)):
            mine[j] = inj[j] - value

    other = p - 1 + 2 * odd
    for row in range(rows):
        near_load(row).wait()
    load_inj.wait()
    load_inv.wait()
    await_halo(soon, side, mate)

    @pl.when(same)
    def _():
        send_rows(beside, soon, side)
        await_halo(late, 1 - side, other)
        send_rows(cross, late, 1 - side)
        keep_rows(soon, side)

    @pl.when(jnp.logical_not(same))
    def _():
        send_rows(cross, soon, side)
        await_halo(late, 1 - side, other)
        send_rows(beside, late, 1 - side)
        keep_rows(late, 1 - side)

    for zs in nearest:
        pltpu.make_async_remote_copy(
            src_ref=arriving.at[zs],
            dst_ref=arriving.at[zs],
            send_sem=part_send.at[zs],
            recv_sem=part_recv.at[zs],
            device_id=(p, zs),
            device_id_type=MESH,
        ).wait_recv()
    residual = mine[...]
    for zs in nearest:
        residual = residual - arriving[zs].astype(jnp.float32)
    res[...] = residual
    write_res = pltpu.make_async_copy(res, res_ref, out_sem.at[0])
    write_res.start()
    rounded = residual.astype(jnp.bfloat16)
    for j in range(owned):
        cor[j] = lax.dot_general(
            rounded[j], inv[j], NT, preferred_element_type=jnp.float32
        )
    write_cor = pltpu.make_async_copy(cor, cor_ref, out_sem.at[1])
    write_cor.start()
    write_res.wait()
    write_cor.wait()
    parts = [part_copy(target) for target in others]
    for copy in gathers + coef_copies + parts:
        copy.wait_send()
    for ok, copy in halos:

        @pl.when(ok)
        def _():
            copy.wait_send()


def hand_over(res_in, cor_in, res_out, cor_out, res, cor, sem):
    loads = [
        pltpu.make_async_copy(res_in, res, sem.at[0]),
        pltpu.make_async_copy(cor_in, cor, sem.at[1]),
    ]
    stores = [
        pltpu.make_async_copy(res, res_out, sem.at[2]),
        pltpu.make_async_copy(cor, cor_out, sem.at[3]),
    ]
    for copy in loads:
        copy.start()
    for load, store in zip(loads, stores):
        load.wait()
        store.start()
    for copy in stores:
        copy.wait()


def local(n_prod, n_pre, potentials, injected, near, cols, rowb, colb, ranks, coup, inv):
    owned, scen, panels = potentials.shape
    rows = near.shape[0]
    out = jax.ShapeDtypeStruct(injected.shape, jnp.float32)
    anywhere = pl.BlockSpec(memory_space=pltpu.HBM)
    scalars = pl.BlockSpec(memory_space=pltpu.SMEM)
    dma = pltpu.SemaphoreType.DMA
    blocks = rows + owned
    residual, corrected = pl.pallas_call(
        functools.partial(kernel, n_prod, n_pre),
        out_shape=(out, out),
        in_specs=[
            anywhere,
            anywhere,
            anywhere,
            scalars,
            anywhere,
            anywhere,
            scalars,
            anywhere,
            anywhere,
        ],
        out_specs=(anywhere, anywhere),
        scratch_shapes=[
            pltpu.VMEM((rows, scen, panels), jnp.bfloat16),
            pltpu.VMEM((rows // 2, scen, panels), jnp.bfloat16),
            pltpu.VMEM((rows // 2, scen, panels), jnp.bfloat16),
            pltpu.VMEM(injected.shape, jnp.float32),
            pltpu.VMEM((rows, panels, panels), jnp.bfloat16),
            pltpu.VMEM(rowb.shape, jnp.bfloat16),
            pltpu.VMEM(colb.shape, jnp.bfloat16),
            pltpu.VMEM(coup.shape, jnp.bfloat16),
            pltpu.VMEM(inv.shape, jnp.bfloat16),
            pltpu.VMEM((n_prod, scen, 128), jnp.bfloat16),
            pltpu.VMEM((rows, scen, panels), jnp.float32),
            pltpu.VMEM(injected.shape, jnp.float32),
            pltpu.VMEM(injected.shape, jnp.float32),
            pltpu.VMEM(injected.shape, jnp.float32),
            pltpu.VMEM((n_pre, owned, scen, panels), jnp.bfloat16),
            pltpu.VMEM((n_pre, owned, scen, panels), jnp.bfloat16),
            dma((6,)),
            dma((rows,)),
            dma((n_pre,)),
            dma((n_pre,)),
            dma((n_pre,)),
            dma((n_pre,)),
            dma((n_prod,)),
            dma((n_prod,)),
            dma((n_pre,)),
            dma((n_pre,)),
            dma((2,)),
        ],
        compiler_params=pltpu.CompilerParams(
            collective_id=0, has_side_effects=True, vmem_limit_bytes=63 * 2**20
        ),
        cost_estimate=pl.CostEstimate(
            flops=2 * blocks * scen * panels * panels,
            bytes_accessed=2 * blocks * panels * panels,
            transcendentals=0,
        ),
    )(potentials, injected, near, cols.reshape(rows), rowb, colb, ranks, coup, inv)
    return pl.pallas_call(
        hand_over,
        out_shape=(out, out),
        in_specs=[anywhere, anywhere],
        out_specs=(anywhere, anywhere),
        scratch_shapes=[
            pltpu.VMEM(injected.shape, jnp.float32),
            pltpu.VMEM(injected.shape, jnp.float32),
            dma((4,)),
        ],
        compiler_params=pltpu.CompilerParams(vmem_limit_bytes=63 * 2**20),
    )(residual, corrected)


def solution(mesh):
    return jax.shard_map(
        functools.partial(local, mesh.shape["prod"], mesh.shape["pre"]),
        mesh=mesh,
        in_specs=(
            P(("prod", "pre"), None, None),
            P(("prod", "pre"), None, None),
            P("prod", "pre", None, None),
            P("prod", "pre"),
            P("prod", None, None),
            P(("prod", "pre"), None, None),
            P(("prod", "pre")),
            P("prod", None, "pre"),
            P(("prod", "pre"), None, None),
        ),
        out_specs=(P(("prod", "pre"), None, None), P(("prod", "pre"), None, None)),
        check_vma=False,
    )
```

profile of v0, /device:TPU:0, one launch (start us, length us, event | category | flops | bytes accessed | tf_op | source)
XLA Modules:
  0.0 25.0 jit_solution(1690993868334718999)
XLA Ops:
  0.6 22.7 %shard_map.104 = (f32[4,16,512]{2,1,0:T(8,128)}, f32[4,16,512]{2,1,0:T(8,128)}) custom-call(bf16[4,16,512]{2,1,0:T(8,128)(2,1)} %pot_hbm.1, f32[4,16,512]{2,1,0:T(8,128)} %inj_hbm.1, bf16[16,1,512,512]{3,2,1,0:T(8,128)(2,1)} %near_hbm.1, s32[16]{0:T(128)} %bitcast.1, bf16[16,16,512]{2,1,0:T(8,128)(2,1)} %rowb_hbm.1, bf16[4,16,512]{2,1,0:T(8,128)(2,1)} %colb_hbm.1, ...), custom_call_target="tpu_custom_call" | custom-call | flops 167772160 | bytes 10485760 | tf_op jit(solution)/shard_map/pallas_call | solution.py:357
  23.3 1.7 %shard_map.105 = (f32[4,16,512]{2,1,0:T(8,128)}, f32[4,16,512]{2,1,0:T(8,128)}) custom-call(f32[4,16,512]{2,1,0:T(8,128)} %get-tuple-element.4.res_in, f32[4,16,512]{2,1,0:T(8,128)} %get-tuple-element.5.cor_in), custom_call_target="tpu_custom_call" | custom-call | tf_op jit(solution)/shard_map/pallas_call | solution.py:410
where the time goes:
time: 25.1 us; the launch traced here: 25 us
  Pallas kernels  24.3 us (97%)
  between operations  0.64 us (3%)
    pallas_call x1, Pallas kernels, local(): pl.pallas_call(functools.partial(kernel, n_prod, n_pre), out_shape=(out,...  22.7 us
    pallas_call x1, Pallas kernels, local(): pl.pallas_call(hand_over, out_shape=(out, out), in_specs=[anywhere, anywh...  1.66 us

commit v1 on v0

--- a/solution.py
+++ b/solution.py
@@ -26,8 +26,8 @@
     res_ref,
     cor_ref,
     group,
-    soon,
-    late,
+    early,
+    later,
     inj,
     near,
     rowb,
@@ -37,8 +37,6 @@
     coef,
     far,
     mine,
-    res,
-    cor,
     sending,
     arriving,
     load_sem,
@@ -51,7 +49,6 @@
     coef_recv,
     part_send,
     part_recv,
-    out_sem,
 ):
     owned, scen, panels = pot_hbm.shape
     rows = near_hbm.shape[0]
@@ -102,8 +99,6 @@
         gathers[-1].start()
 
     halos = []
-    odd = p % 2
-    mate, side = p + 1 - 2 * odd, 1 - odd
 
     def halo_copy(buffer, zs, send, source, to):
         return pltpu.make_async_remote_copy(
@@ -115,40 +110,38 @@
             device_id_type=MESH,
         )
 
-    def forward(zs, index, source=None):
+    def forward(zs, index, buffer, source=None):
         source = slot(zs) if source is None else source
         to = jnp.where(zs < half, p - 1, p + 1)
-        near_by = (z >= 1) & (to == mate)
-        far_off = (z >= 1) & (to != mate) & (to >= 0) & (to < n_prod)
-        for ok, buffer in ((near_by, soon), (far_off, late)):
-            copy = halo_copy(buffer, zs, index, source, to)
-
-            @pl.when(ok)
-            def _():
-                copy.start()
-
-            halos.append((ok, copy))
-
-    def await_halo(buffer, upper, from_device):
-        @pl.when((z >= 1) & (from_device >= 0) & (from_device < n_prod))
+        ok = (z >= 1) & (to >= 0) & (to < n_prod)
+        copy = halo_copy(buffer, zs, index, source, to)
+
+        @pl.when(ok)
+        def _():
+            copy.start()
+
+        halos.append((ok, copy))
+
+    def await_halo(buffer, upper):
+        source = p - 1 + 2 * upper
+
+        @pl.when((z >= 1) & (source >= 0) & (source < n_prod))
         def _():
             for e in range(half):
                 zs = (1 - upper) * half + e
-                halo_copy(buffer, zs, 0, slot(zs), from_device).wait_recv()
-
-    forward(z, 0, pot_hbm)
+                halo_copy(buffer, zs, 0, slot(zs), source).wait_recv()
+
+    forward(z, 0, early, pot_hbm)
     load_coup.start()
     load_rowb.start()
-    same = (side == high) & (z >= 1)
     cross, beside = others[:half], others[half:]
-    orders = (cross + beside + [z], beside + cross + [z])
 
     def near_load(row):
         return pltpu.make_async_copy(near_hbm.at[row, 0], near.at[row], near_sem.at[row])
 
-    for first, second in zip(*orders):
+    for target in others + [z]:
         for j in range(owned):
-            near_load(jnp.where(same, second, first) * owned + j).start()
+            near_load(target * owned + j).start()
     load_inj.start()
     load_inv.start()
     load_pot.wait()
@@ -194,9 +187,9 @@
             device_id=(p, zs),
             device_id_type=MESH,
         ).wait_recv()
-        forward(zs, index + 1)
-
-    for index in range(n_pre - 1):
+        forward(zs, index + 1, early if index < half - 1 else later)
+
+    for index in range(half - 1):
         collect(index)
 
     for e in range(1, n_prod):
@@ -273,27 +266,17 @@
         for j, value in enumerate(rows_of(z, buffer, upper)):
             mine[j] = inj[j] - value
 
-    other = p - 1 + 2 * odd
     for row in range(rows):
         near_load(row).wait()
     load_inj.wait()
     load_inv.wait()
-    await_halo(soon, side, mate)
-
-    @pl.when(same)
-    def _():
-        send_rows(beside, soon, side)
-        await_halo(late, 1 - side, other)
-        send_rows(cross, late, 1 - side)
-        keep_rows(soon, side)
-
-    @pl.when(jnp.logical_not(same))
-    def _():
-        send_rows(cross, soon, side)
-        await_halo(late, 1 - side, other)
-        send_rows(beside, late, 1 - side)
-        keep_rows(late, 1 - side)
-
+    for index in range(half - 1, n_pre - 1):
+        collect(index)
+    await_halo(early, 1 - high)
+    send_rows(cross, early, 1 - high)
+    await_halo(later, high)
+    send_rows(beside, later, high)
+    keep_rows(later, high)
     for zs in nearest:
         pltpu.make_async_remote_copy(
             src_ref=arriving.at[zs],
@@ -306,18 +289,12 @@
     residual = mine[...]
     for zs in nearest:
         residual = residual - arriving[zs].astype(jnp.float32)
-    res[...] = residual
-    write_res = pltpu.make_async_copy(res, res_ref, out_sem.at[0])
-    write_res.start()
+    res_ref[...] = residual
     rounded = residual.astype(jnp.bfloat16)
     for j in range(owned):
-        cor[j] = lax.dot_general(
+        cor_ref[j] = lax.dot_general(
             rounded[j], inv[j], NT, preferred_element_type=jnp.float32
         )
-    write_cor = pltpu.make_async_copy(cor, cor_ref, out_sem.at[1])
-    write_cor.start()
-    write_res.wait()
-    write_cor.wait()
     parts = [part_copy(target) for target in others]
     for copy in gathers + coef_copies + parts:
         copy.wait_send()
@@ -328,20 +305,13 @@
             copy.wait_send()
 
 
-def hand_over(res_in, cor_in, res_out, cor_out, res, cor, sem):
-    loads = [
-        pltpu.make_async_copy(res_in, res, sem.at[0]),
-        pltpu.make_async_copy(cor_in, cor, sem.at[1]),
+def hand_over(res_in, cor_in, res_out, cor_out, sem):
+    stores = [
+        pltpu.make_async_copy(res_in, res_out, sem.at[0]),
+        pltpu.make_async_copy(cor_in, cor_out, sem.at[1]),
     ]
-    stores = [
-        pltpu.make_async_copy(res, res_out, sem.at[2]),
-        pltpu.make_async_copy(cor, cor_out, sem.at[3]),
-    ]
-    for copy in loads:
+    for copy in stores:
         copy.start()
-    for load, store in zip(loads, stores):
-        load.wait()
-        store.start()
     for copy in stores:
         copy.wait()
 
@@ -351,12 +321,14 @@
     rows = near.shape[0]
     out = jax.ShapeDtypeStruct(injected.shape, jnp.float32)
     anywhere = pl.BlockSpec(memory_space=pltpu.HBM)
+    vmem = pl.BlockSpec(memory_space=pltpu.VMEM)
+    held = pltpu.VMEM(injected.shape, jnp.float32)
     scalars = pl.BlockSpec(memory_space=pltpu.SMEM)
     dma = pltpu.SemaphoreType.DMA
     blocks = rows + owned
     residual, corrected = pl.pallas_call(
         functools.partial(kernel, n_prod, n_pre),
-        out_shape=(out, out),
+        out_shape=(held, held),
         in_specs=[
             anywhere,
             anywhere,
@@ -368,7 +340,7 @@
             anywhere,
             anywhere,
         ],
-        out_specs=(anywhere, anywhere),
+        out_specs=(vmem, vmem),
         scratch_shapes=[
             pltpu.VMEM((rows, scen, panels), jnp.bfloat16),
             pltpu.VMEM((rows // 2, scen, panels), jnp.bfloat16),
@@ -382,8 +354,6 @@
             pltpu.VMEM((n_prod, scen, 128), jnp.bfloat16),
             pltpu.VMEM((rows, scen, panels), jnp.float32),
             pltpu.VMEM(injected.shape, jnp.float32),
-            pltpu.VMEM(injected.shape, jnp.float32),
-            pltpu.VMEM(injected.shape, jnp.float32),
             pltpu.VMEM((n_pre, owned, scen, panels), jnp.bfloat16),
             pltpu.VMEM((n_pre, owned, scen, panels), jnp.bfloat16),
             dma((6,)),
@@ -396,7 +366,6 @@
             dma((n_prod,)),
             dma((n_pre,)),
             dma((n_pre,)),
-            dma((2,)),
         ],
         compiler_params=pltpu.CompilerParams(
             collective_id=0, has_side_effects=True, vmem_limit_bytes=63 * 2**20
@@ -410,14 +379,10 @@
     return pl.pallas_call(
         hand_over,
         out_shape=(out, out),
-        in_specs=[anywhere, anywhere],
+        in_specs=[vmem, vmem],
         out_specs=(anywhere, anywhere),
-        scratch_shapes=[
-            pltpu.VMEM(injected.shape, jnp.float32),
-            pltpu.VMEM(injected.shape, jnp.float32),
-            dma((4,)),
-        ],
-        compiler_params=pltpu.CompilerParams(vmem_limit_bytes=63 * 2**20),
+        scratch_shapes=[dma((2,))],
+        compiler_params=pltpu.CompilerParams(vmem_limit_bytes=8 * 2**20),
     )(residual, corrected)
 
 

time: 25.1 us -> 23.8 us (0.948)
  Pallas kernels: 24.3 us -> 23 us
    pallas_call x2, Pallas kernels: 24.3 us -> 23 us  [the longest x1 22.3 us: local(): pl.pallas_call(functools.partial(kernel, n_prod, n_pre), out_shape=(held,...]
where the time goes in v1:
time: 23.8 us; the launch traced here: 23.6 us
  Pallas kernels  23 us (97%)
  between operations  0.64 us (3%)
    pallas_call x1, Pallas kernels, local(): pl.pallas_call(functools.partial(kernel, n_prod, n_pre), out_shape=(held,...  22.3 us
    pallas_call x1, Pallas kernels, local(): pl.pallas_call(hand_over, out_shape=(out, out), in_specs=[vmem, vmem], ou...  0.72 us

profile of v1, /device:TPU:0, one launch (start us, length us, event | category | flops | bytes accessed | tf_op | source)
XLA Modules:
  0.0 23.6 jit_solution(338835745405754349)
XLA Ops:
  0.6 22.3 %shard_map.104 = (f32[4,16,512]{2,1,0:T(8,128)S(1)}, f32[4,16,512]{2,1,0:T(8,128)S(1)}) custom-call(bf16[4,16,512]{2,1,0:T(8,128)(2,1)} %pot_hbm.1, f32[4,16,512]{2,1,0:T(8,128)} %inj_hbm.1, bf16[16,1,512,512]{3,2,1,0:T(8,128)(2,1)} %near_hbm.1, s32[16]{0:T(128)} %bitcast.1, bf16[16,16,512]{2,1,0:T(8,128)(2,1)} %rowb_hbm.1, bf16[4,16,512]{2,1,0:T(8,128)(2,1)} %colb_hbm.1, ...), custom_call_target="tpu_custom_call" | custom-call | flops 167772160 | bytes 10485760 | tf_op jit(solution)/shard_map/pallas_call | solution.py:329
  22.9 0.7 %shard_map.105 = (f32[4,16,512]{2,1,0:T(8,128)}, f32[4,16,512]{2,1,0:T(8,128)}) custom-call(f32[4,16,512]{2,1,0:T(8,128)S(1)} %get-tuple-element.4.res_in, f32[4,16,512]{2,1,0:T(8,128)S(1)} %get-tuple-element.5.cor_in), custom_call_target="tpu_custom_call" | custom-call | tf_op jit(solution)/shard_map/pallas_call | solution.py:379

commit v2 on v1

--- a/solution.py
+++ b/solution.py
@@ -189,7 +189,7 @@
         ).wait_recv()
         forward(zs, index + 1, early if index < half - 1 else later)
 
-    for index in range(half - 1):
+    for index in range(n_pre - 1):
         collect(index)
 
     for e in range(1, n_prod):
@@ -270,8 +270,6 @@
         near_load(row).wait()
     load_inj.wait()
     load_inv.wait()
-    for index in range(half - 1, n_pre - 1):
-        collect(index)
     await_halo(early, 1 - high)
     send_rows(cross, early, 1 - high)
     await_halo(later, high)

time: 23.8 us -> 23.9 us (level)
  no operation moved by 1% of the time
where the time goes in v2:
time: 23.9 us; the launch traced here: 23.8 us
  Pallas kernels  23.1 us (97%)
  between operations  0.64 us (3%)
    pallas_call x1, Pallas kernels, local(): pl.pallas_call(functools.partial(kernel, n_prod, n_pre), out_shape=(held,...  22.4 us
    pallas_call x1, Pallas kernels, local(): pl.pallas_call(hand_over, out_shape=(out, out), in_specs=[vmem, vmem], ou...  0.72 us

profile of v2, /device:TPU:0, one launch (start us, length us, event | category | flops | bytes accessed | tf_op | source)
XLA Modules:
  0.0 23.8 jit_solution(6223164733504319736)
XLA Ops:
  0.6 22.4 %shard_map.104 = (f32[4,16,512]{2,1,0:T(8,128)S(1)}, f32[4,16,512]{2,1,0:T(8,128)S(1)}) custom-call(bf16[4,16,512]{2,1,0:T(8,128)(2,1)} %pot_hbm.1, f32[4,16,512]{2,1,0:T(8,128)} %inj_hbm.1, bf16[16,1,512,512]{3,2,1,0:T(8,128)(2,1)} %near_hbm.1, s32[16]{0:T(128)} %bitcast.1, bf16[16,16,512]{2,1,0:T(8,128)(2,1)} %rowb_hbm.1, bf16[4,16,512]{2,1,0:T(8,128)(2,1)} %colb_hbm.1, ...), custom_call_target="tpu_custom_call" | custom-call | flops 167772160 | bytes 10485760 | tf_op jit(solution)/shard_map/pallas_call | solution.py:327
  23.0 0.7 %shard_map.105 = (f32[4,16,512]{2,1,0:T(8,128)}, f32[4,16,512]{2,1,0:T(8,128)}) custom-call(f32[4,16,512]{2,1,0:T(8,128)S(1)} %get-tuple-element.4.res_in, f32[4,16,512]{2,1,0:T(8,128)S(1)} %get-tuple-element.5.cor_in), custom_call_target="tpu_custom_call" | custom-call | tf_op jit(solution)/shard_map/pallas_call | solution.py:377

commit v3 on v1

--- a/solution.py
+++ b/solution.py
@@ -82,71 +82,8 @@
         pl.semaphore_signal(
             barrier, inc=1, device_id=((p + e) % n_prod, z), device_id_type=MESH
         )
-    pl.semaphore_wait(barrier, n_pre - 1 + n_prod - 1)
-
-    gathers = []
-    for e, target in enumerate(others):
-        gathers.append(
-            pltpu.make_async_remote_copy(
-                src_ref=pot_hbm,
-                dst_ref=slot(z),
-                send_sem=gather_send.at[e],
-                recv_sem=gather_recv.at[z],
-                device_id=(p, target),
-                device_id_type=MESH,
-            )
-        )
-        gathers[-1].start()
-
-    halos = []
-
-    def halo_copy(buffer, zs, send, source, to):
-        return pltpu.make_async_remote_copy(
-            src_ref=source,
-            dst_ref=buffer.at[pl.ds(zs % half * owned, owned)],
-            send_sem=halo_send.at[send],
-            recv_sem=halo_recv.at[zs],
-            device_id=(to, z),
-            device_id_type=MESH,
-        )
-
-    def forward(zs, index, buffer, source=None):
-        source = slot(zs) if source is None else source
-        to = jnp.where(zs < half, p - 1, p + 1)
-        ok = (z >= 1) & (to >= 0) & (to < n_prod)
-        copy = halo_copy(buffer, zs, index, source, to)
-
-        @pl.when(ok)
-        def _():
-            copy.start()
-
-        halos.append((ok, copy))
-
-    def await_halo(buffer, upper):
-        source = p - 1 + 2 * upper
-
-        @pl.when((z >= 1) & (source >= 0) & (source < n_prod))
-        def _():
-            for e in range(half):
-                zs = (1 - upper) * half + e
-                halo_copy(buffer, zs, 0, slot(zs), source).wait_recv()
-
-    forward(z, 0, early, pot_hbm)
-    load_coup.start()
-    load_rowb.start()
-    cross, beside = others[:half], others[half:]
-
-    def near_load(row):
-        return pltpu.make_async_copy(near_hbm.at[row, 0], near.at[row], near_sem.at[row])
-
-    for target in others + [z]:
-        for j in range(owned):
-            near_load(target * owned + j).start()
-    load_inj.start()
-    load_inv.start()
     load_pot.wait()
     load_colb.wait()
-
     pot = group[pl.ds(z * owned, owned)].reshape(owned * scen, panels)
     basis = colb[...].reshape(width, panels)
     products = lax.dot_general(
@@ -163,6 +100,7 @@
         keep = here & (inner // rank_cap == j) & (inner % rank_cap < ranks_ref[j])
         mine_coef = jnp.where(keep, products[j * scen : (j + 1) * scen], mine_coef)
     coef[p] = mine_coef.astype(jnp.bfloat16)
+    pl.semaphore_wait(barrier, n_pre - 1 + n_prod - 1)
     coef_copies = []
     for e in range(1, n_prod):
         coef_copies.append(
@@ -176,6 +114,68 @@
             )
         )
         coef_copies[-1].start()
+
+
+    gathers = []
+    for e, target in enumerate(others):
+        gathers.append(
+            pltpu.make_async_remote_copy(
+                src_ref=pot_hbm,
+                dst_ref=slot(z),
+                send_sem=gather_send.at[e],
+                recv_sem=gather_recv.at[z],
+                device_id=(p, target),
+                device_id_type=MESH,
+            )
+        )
+        gathers[-1].start()
+
+    halos = []
+
+    def halo_copy(buffer, zs, send, source, to):
+        return pltpu.make_async_remote_copy(
+            src_ref=source,
+            dst_ref=buffer.at[pl.ds(zs % half * owned, owned)],
+            send_sem=halo_send.at[send],
+            recv_sem=halo_recv.at[zs],
+            device_id=(to, z),
+            device_id_type=MESH,
+        )
+
+    def forward(zs, index, buffer, source=None):
+        source = slot(zs) if source is None else source
+        to = jnp.where(zs < half, p - 1, p + 1)
+        ok = (z >= 1) & (to >= 0) & (to < n_prod)
+        copy = halo_copy(buffer, zs, index, source, to)
+
+        @pl.when(ok)
+        def _():
+            copy.start()
+
+        halos.append((ok, copy))
+
+    def await_halo(buffer, upper):
+        source = p - 1 + 2 * upper
+
+        @pl.when((z >= 1) & (source >= 0) & (source < n_prod))
+        def _():
+            for e in range(half):
+                zs = (1 - upper) * half + e
+                halo_copy(buffer, zs, 0, slot(zs), source).wait_recv()
+
+    forward(z, 0, early, pot_hbm)
+    load_coup.start()
+    load_rowb.start()
+    cross, beside = others[:half], others[half:]
+
+    def near_load(row):
+        return pltpu.make_async_copy(near_hbm.at[row, 0], near.at[row], near_sem.at[row])
+
+    for target in others + [z]:
+        for j in range(owned):
+            near_load(target * owned + j).start()
+    load_inj.start()
+    load_inv.start()
 
     def collect(index):
         zs = nearest[index]

time: 23.8 us -> 23.8 us (level)
  no operation moved by 1% of the time
where the time goes in v3:
time: 23.8 us; the launch traced here: 23.6 us
  Pallas kernels  23 us (97%)
  between operations  0.64 us (3%)
    pallas_call x1, Pallas kernels, local(): pl.pallas_call(functools.partial(kernel, n_prod, n_pre), out_shape=(held,...  22.3 us
    pallas_call x1, Pallas kernels, local(): pl.pallas_call(hand_over, out_shape=(out, out), in_specs=[vmem, vmem], ou...  0.72 us

profile of v3, /device:TPU:0, one launch (start us, length us, event | category | flops | bytes accessed | tf_op | source)
XLA Modules:
  0.0 23.6 jit_solution(17957412912050602507)
XLA Ops:
  0.6 22.3 %shard_map.104 = (f32[4,16,512]{2,1,0:T(8,128)S(1)}, f32[4,16,512]{2,1,0:T(8,128)S(1)}) custom-call(bf16[4,16,512]{2,1,0:T(8,128)(2,1)} %pot_hbm.1, f32[4,16,512]{2,1,0:T(8,128)} %inj_hbm.1, bf16[16,1,512,512]{3,2,1,0:T(8,128)(2,1)} %near_hbm.1, s32[16]{0:T(128)} %bitcast.1, bf16[16,16,512]{2,1,0:T(8,128)(2,1)} %rowb_hbm.1, bf16[4,16,512]{2,1,0:T(8,128)(2,1)} %colb_hbm.1, ...), custom_call_target="tpu_custom_call" | custom-call | flops 167772160 | bytes 10485760 | tf_op jit(solution)/shard_map/pallas_call | solution.py:329
  22.9 0.7 %shard_map.105 = (f32[4,16,512]{2,1,0:T(8,128)}, f32[4,16,512]{2,1,0:T(8,128)}) custom-call(f32[4,16,512]{2,1,0:T(8,128)S(1)} %get-tuple-element.4.res_in, f32[4,16,512]{2,1,0:T(8,128)S(1)} %get-tuple-element.5.cor_in), custom_call_target="tpu_custom_call" | custom-call | tf_op jit(solution)/shard_map/pallas_call | solution.py:379
